TPU v7x, 256 devices: a whole 4x4x8 slice. The times are simulated.
256 devices in a mesh: rep: 8 (over z_hi, core), wide: 32 (over z_lo, y, x).
Axes of the slice: x: 4, y: 4, z: 8 (z_hi: 4, z_lo: 2; z = z_hi * 2 + z_lo), core: 2. Of those that a mesh axis runs over, the one named last changes fastest.
Arguments:
- pool: bfloat16 [8192, 4096], P(('rep', 'wide')), may hold values from -6 to 6
- ids: int32 [6144], P('rep'), may hold values from 0 to 1023
- block_rows: int32 [2], replicated, may hold values from 0 to 15
- enc_weight: bfloat16 [4096, 32768], P(None, 'wide'), may hold values from -0.09375 to 0.09375
- enc_bias: float32 [32768], P('wide'), may hold values from -3 to 3
- dec_bias: float32 [4096], replicated, may hold values from -3 to 3
Outputs:
- gram: float32 [4096, 32768], P('rep', 'wide')
All inputs are finite; a program needn't handle non-finite values.
Results may differ from a plain program's by a relative error of at most 0.0003.
Values may be sent and summed in bfloat16 or wider, within the bound.
A program may use at most 128 MiB of HBM per device.

v0:
```python
import jax
import jax.numpy as jnp
from jax import lax
from jax.sharding import PartitionSpec as P

BLOCK = 2048
NB = 2


def from_root(value, axis, source):
    kept = jnp.where(lax.axis_index(axis) == source, value, 0).astype(value.dtype)
    return lax.psum(kept, axis)


def local(pool, ids, block_rows, enc_weight, enc_bias, dec_bias):
    tok_count = ids.shape[0]
    table = lax.all_gather(pool, "wide", axis=0, tiled=True)
    residual = jnp.take(table, ids, axis=0)
    values = residual.astype(jnp.float32)
    power = jnp.mean(values * values, axis=-1, keepdims=True)
    centered = (values * lax.rsqrt(power + 1e-06) - dec_bias).astype(jnp.bfloat16)
    before = jnp.dot(centered, enc_weight, preferred_element_type=jnp.float32) + enc_bias
    codes = jnp.maximum(before, 0.0).astype(jnp.bfloat16)
    panel = codes.shape[1]
    piece_width = min(BLOCK, panel)
    pieces_per_block = max(1, BLOCK // panel)
    gathered = []
    for block in range(NB):
        for inner in range(pieces_per_block):
            first = block_rows[block] * BLOCK + inner * piece_width
            owner = first // panel
            gathered.append(from_root(codes, "wide", owner))
    chosen = jnp.concatenate(gathered, axis=1)
    scale_back = 1.0 / float(tok_count * lax.axis_size("rep"))
    panel_sum = lax.dot_general(
        chosen, codes, (((0,), (0,)), ((), ())), preferred_element_type=jnp.float32
    )
    summed = lax.psum_scatter(panel_sum, "rep", scatter_dimension=0, tiled=True)
    return summed * scale_back


def solution(mesh):
    placed = (P(("rep", "wide"), None), P("rep"), P(), P(None, "wide"), P("wide"), P())
    return jax.shard_map(
        local, mesh=mesh, in_specs=placed, out_specs=P("rep", "wide"), check_vma=False
    )
```

profile of v0, /device:TPU:2, one launch (start us, length us, event | category | flops | bytes accessed | tf_op | source)
XLA Modules:
  0.0 763.5 jit_solution(12737434678435332426)
XLA Ops:
  6.5 0.0 all-gather.2.cloned.1.call-start
  6.5 0.7 all-gather.2.cloned.1.call-update
  7.3 0.0 all-reduce.3.cloned.1.call-start
  7.3 1.4 fusion.19
  10.1 0.7 compare_select_fusion
  10.8 0.7 compare_and_fusion
  11.5 170.7 %all-gather.2.cloned.1.call-done = bf16[1024,4096]{1,0:T(8,128)(2,1)} async-done(((bf16[32,4096]{1,0:T(8,128)(2,1)}), bf16[1024,4096]{1,0:T(8,128)(2,1)}) %all-gather.2.cloned.1.call-update) | async-done | bytes 8388624 | tf_op jit(solution)/shard_map/all_gather | solution.py:17
  182.2 0.0 copy-start.1
  182.2 16.4 %gather_fusion = bf16[768,4096]{1,0:T(8,128)(2,1)} fusion(bf16[1024,4096]{1,0:T(8,128)(2,1)} %all-gather.2.cloned.1.call-done, s32[1024]{0:T(1024)S(1)} %pad_clamp_fusion), kind=kCustom, calls=%fused_computation | custom fusion | bytes 12585984 | tf_op jit(solution)/shard_map/jit(_take)/gather | solution.py:18
  198.6 0.0 copy-start
  198.6 0.0 copy-start.2
  198.6 4.7 fusion
  203.3 0.0 copy-done.1
  203.3 0.0 copy-done
  203.4 0.0 copy-done.2
  203.4 12.5 %broadcast_select_fusion.5 = (bf16[768,1024]{1,0:T(8,128)(2,1)}, bf16[768,1024]{1,0:T(8,128)(2,1)}, bf16[768,1024]{1,0:T(8,128)(2,1)}, bf16[768,1024]{1,0:T(8,128)(2,1)}, bf16[768,1024]{1,0:T(8,128)(2,1)S(1)}) fusion(pred[]{:T(512)S(6)} %eq.12, pred[]{:T(512)S(6)} %eq.15, pred[]{:T(512)S(6)} %eq.14, pred[]{:T(512)S(6)} %eq.13, f32[1024]{0:T(1024)S(1)} %copy-done.2, ...), kind=kOutput, calls=%fused_computation.22 | convolution fusion | flops 6463684608 | bytes 22568708 | tf_op jit(solution)/shard_map/dot_general | solution.py:22
  215.9 0.0 all-reduce.3.cloned.1.call-update
  215.9 0.2 reduce-scatter.2.cloned.1.call-start
  216.1 339.7 %all-reduce.3.cloned.1.call-done = (bf16[768,1024]{1,0:T(8,128)(2,1)}, bf16[768,1024]{1,0:T(8,128)(2,1)}, bf16[768,1024]{1,0:T(8,128)(2,1)}, bf16[768,1024]{1,0:T(8,128)(2,1)}) async-done(((bf16[768,1024]{1,0:T(8,128)(2,1)}, bf16[768,1024]{1,0:T(8,128)(2,1)}, bf16[768,1024]{1,0:T(8,128)(2,1)}, bf16[768,1024]{1,0:T(8,128)(2,1)}), (bf16[768,1024]{1,0:T(8,128)(2,1)}, bf16[768,1024]{1,0:T(8,128)(2,1)}, ...) | async-done | bytes 6291472 | tf_op jit(solution)/shard_map/psum | solution.py:12
  555.8 15.3 %fusion.5 = f32[4096,1024]{1,0:T(8,128)} fusion(bf16[768,1024]{1,0:T(8,128)(2,1)S(1)} %get-tuple-element.15, bf16[768,1024]{1,0:T(8,128)(2,1)} %get-tuple-element.5, bf16[768,1024]{1,0:T(8,128)(2,1)} %get-tuple-element.6, bf16[768,1024]{1,0:T(8,128)(2,1)} %get-tuple-element.7, bf16[768,1024]{1,0:T(8,128)(2,1)} %get-tuple-element.8), kind=kOutput, calls=%fused_computation.7 | convolution fusion | flops 6467616768 | bytes 24641536 | tf_op jit(solution)/shard_map/dot_general | solution.py:35
  571.2 0.0 reduce-scatter.2.cloned.1.call-update
  571.2 182.5 %reduce-scatter.2.cloned.1.call-done = f32[512,1024]{1,0:T(8,128)} async-done(((f32[4096,1024]{1,0:T(8,128)}), f32[512,1024]{1,0:T(8,128)}) %reduce-scatter.2.cloned.1.call-update) | async-done | bytes 2097168 | tf_op jit(solution)/shard_map/reduce_scatter | solution.py:38
  753.7 3.3 broadcast_multiply_fusion
  (2 shorter events, 0.0 us)
Async XLA Ops:
  6.5 175.6 %all-gather.2.cloned.1.call-start = ((), (), s32[]{:S(2)}) async-start(), calls=%async_computation.1 | async-start | bytes 8650752 | tf_op jit(solution)/shard_map/all_gather | solution.py:17
  7.3 548.6 %all-reduce.3.cloned.1.call-start = ((), (), s32[]{:S(2)}) async-start(), calls=%async_computation.3 | async-start | bytes 12582912 | tf_op jit(solution)/shard_map/psum | solution.py:12
  182.2 21.2 %copy-start.1 = (f32[4096]{0:T(1024)S(1)}, f32[4096]{0:T(1024)}, u32[]{:S(2)}) copy-start(f32[4096]{0:T(1024)} %param.11) | copy-start | bytes 49156
  198.6 4.7 copy-start
  198.6 4.8 copy-start.2
  215.9 537.8 %reduce-scatter.2.cloned.1.call-start = ((), (), s32[]{:S(2)}) async-start(), calls=%async_computation.2 | async-start | bytes 18874368 | tf_op jit(solution)/shard_map/reduce_scatter | solution.py:38
Sparse Core Ops, SparseCore 0:
  9.1 172.9 all-gather.1
  216.0 339.7 all-reduce.2
  571.3 182.3 reduce-scatter.1
where the time goes:
time: 765 us; the launch traced here: 764 us
  waiting for transfers between devices  694 us (91%)
  matrix products  27.9 us (4%)
  local copies, waits for them, and re-layouts  17.8 us (2%)
  between operations  14.6 us (2%)
  other arithmetic  9.4 us (1%)
    psum x1, waiting for transfers between devices, from_root(): return lax.psum(kept, axis)  340 us
    reduce_scatter x1, waiting for transfers between devices, local(): summed = lax.psum_scatter(panel_sum, 'rep', scatter_dimension=0, tiled=True)  183 us
    all_gather x1, waiting for transfers between devices, local(): table = lax.all_gather(pool, 'wide', axis=0, tiled=True)  171 us
    gather x1, local copies, waits for them, and re-layouts, local(): residual = jnp.take(table, ids, axis=0)  16.4 us
    dot_general x1, matrix products, local(): lax.dot_general(chosen, codes, (((0,), (0,)), ((), ())), preferred_elemen...  15.3 us
  transfers between devices with their start and end apart: 3, of which 3 were waited for; matrix products, arithmetic and copies ran while one was open for 0% of the time, Pallas kernels for 0%

commit v1 on v0

v1 whole, which is shorter than its diff:
```python
import functools

import jax
import jax.numpy as jnp
from jax import lax
from jax.experimental import pallas as pl
from jax.experimental.pallas import tpu as pltpu
from jax.sharding import PartitionSpec as P

BLOCK = 2048
D = 4096
TOK = 768
PANEL = 1024
HALF = 512
ROWS = 512
PIECE = 48
CHUNK = 192
MESH = pl.DeviceIdType.MESH
F32 = jnp.float32
BF16 = jnp.bfloat16


def kernel(pool_ref, pos_ref, rows_ref, w_hbm, eb_ref, db_ref, out_ref,
           w_vm, cent, pcodes, codes, a2a, sel, chosen,
           w_sem, ps, pr, cs, cr, as_, ar, rs, rr, zs, zr, fs, fr, ks, kr):
    r = lax.axis_index("rep")
    w = lax.axis_index("wide")
    h, c = r // 2, r % 2
    zl, y, x = w // 16, (w // 4) % 4, w % 4
    sends = []

    def wide_of(zz, yy, xx):
        return zz * 16 + yy * 4 + xx

    def copy(src, dst, ssem, rsem, dev):
        return pltpu.make_async_remote_copy(
            src_ref=src, dst_ref=dst, send_sem=ssem, recv_sem=rsem,
            device_id=dev, device_id_type=MESH)

    def send(src, dst, ssem, rsem, dev):
        d = copy(src, dst, ssem, rsem, dev)
        d.start()
        sends.append(d)

    def arrived(dst, ssem, rsem, dev):
        copy(dst, dst, ssem, rsem, dev).wait_recv()

    w_copy = pltpu.make_async_copy(w_hbm, w_vm, w_sem)
    w_copy.start()

    barrier = pltpu.get_barrier_semaphore()

    def greet_wide(i, carry):
        pl.semaphore_signal(barrier, inc=1, device_id=(r, (w + i) % 32), device_id_type=MESH)
        return carry

    def greet_rep(i, carry):
        pl.semaphore_signal(barrier, inc=1, device_id=((r + i) % 8, w), device_id_type=MESH)
        return carry

    lax.fori_loop(1, 32, greet_wide, 0)
    lax.fori_loop(1, 8, greet_rep, 0)

    for ab in range(2):
        values = pool_ref[ab * 16:(ab + 1) * 16, :].astype(F32)
        power = jnp.mean(values * values, axis=-1, keepdims=True)
        centered = (values * lax.rsqrt(power + 1e-06) - db_ref[...]).astype(BF16)
        if ab == 0:
            cent[0, y, zl, x] = centered
        else:
            cent[1, x, zl, y] = centered

    pl.semaphore_wait(barrier, 38)

    def gather(buf, ss, sr, own_ready, near_ready, far_ready):
        place = ((y, x), (x, y))

        def first(ab, d):
            if ab == 0:
                return (r, wide_of(zl, y, (x + d + 4) % 4))
            return (r, wide_of(zl, (y + d + 4) % 4, x))

        def second(ab, d):
            return first(1 - ab, d)

        other = (r, wide_of(1 - zl, y, x))
        steps = (1, -1)
        for ab in range(2):
            k, m = place[ab]
            own = buf.at[ab, k, zl, m]
            send(own, own, ss.at[ab, 0], sr.at[ab, 0], other)
            for i, d in enumerate(steps):
                send(own, own, ss.at[ab, 1 + i * 2 + zl], sr.at[ab, 1 + i * 2 + zl], first(ab, d))
        for ab in range(2):
            k, m = place[ab]
            got = buf.at[ab, k, 1 - zl, m]
            arrived(got, ss.at[ab, 0], sr.at[ab, 0], other)
            for i, d in enumerate(steps):
                s = 1 + i * 2 + 1 - zl
                send(got, got, ss.at[ab, s], sr.at[ab, s], first(ab, d))
        for ab in range(2):
            k, m = place[ab]
            for i, d in enumerate(steps):
                got = buf.at[ab, k, i, (m - d + 4) % 4]
                s = 1 + i * 2 + i
                arrived(got, ss.at[ab, s], sr.at[ab, s], first(ab, -d))
                send(got, got, ss.at[ab, 5 + i], sr.at[ab, 5 + i], first(ab, d))
        for ab in range(2):
            k, m = place[ab]
            for i, d in enumerate(steps):
                s = 1 + i * 2 + 1 - i
                arrived(buf.at[ab, k, 1 - i, (m - d + 4) % 4], ss.at[ab, s], sr.at[ab, s], first(ab, -d))
        for ab in range(2):
            k, m = place[ab]
            for i, d in enumerate(steps):
                arrived(buf.at[ab, k, i, (m + 2) % 4], ss.at[ab, 5 + i], sr.at[ab, 5 + i], first(ab, -d))
        for z in range(2):
            for ab in range(2):
                k, m = place[ab]
                for i, d in enumerate(steps):
                    part = buf.at[ab, k, z if i == 0 else 1 - z]
                    s = 7 + i * 2 + (z if i == 0 else 1 - z)
                    send(part, part, ss.at[ab, s], sr.at[ab, s], second(ab, d))
        own_ready()
        for ab in range(2):
            k, m = place[ab]
            for i, d in enumerate(steps):
                got = buf.at[ab, (k - d + 4) % 4, i]
                s = 7 + i * 2 + i
                arrived(got, ss.at[ab, s], sr.at[ab, s], second(ab, -d))
                send(got, got, ss.at[ab, 11 + i], sr.at[ab, 11 + i], second(ab, d))
        for i, d in enumerate(steps):
            for ab in range(2):
                k, m = place[ab]
                s = 7 + i * 2 + 1 - i
                arrived(buf.at[ab, (k - d + 4) % 4, 1 - i], ss.at[ab, s], sr.at[ab, s], second(ab, -d))
            near_ready(d)
        for ab in range(2):
            k, m = place[ab]
            for i, d in enumerate(steps):
                arrived(buf.at[ab, (k + 2) % 4, i], ss.at[ab, 11 + i], sr.at[ab, 11 + i], second(ab, -d))
        far_ready()

    def encode(ky, kx):
        def tile(n, carry):
            cols = pl.ds(pl.multiple_of(n * 256, 256), 256)
            lhs = jnp.concatenate(
                [cent[0, ky].reshape(128, D), cent[1, kx].reshape(128, D)], axis=0)
            before = jnp.dot(lhs, w_vm[:, cols], preferred_element_type=F32) + eb_ref[:, cols]
            made = jnp.maximum(before, 0.0).astype(BF16)
            pcodes[pl.ds(pl.multiple_of(ky * 128, 128), 128), cols] = made[:128]
            pcodes[pl.ds(pl.multiple_of(512 + kx * 128, 128), 128), cols] = made[128:]
            return carry

        lax.fori_loop(0, 4, tile, 0)

    def own_ready():
        w_copy.wait()
        encode(y, x)

    gather(cent, ps, pr, own_ready,
           lambda d: encode((y - d + 4) % 4, (x - d + 4) % 4),
           lambda: encode((y + 2) % 4, (x + 2) % 4))

    def pick(q, carry):
        rows = pl.ds(pl.multiple_of(q * CHUNK, CHUNK), CHUNK)
        hot = (pos_ref[rows, :] == lax.broadcasted_iota(jnp.int32, (CHUNK, 1024), 1)).astype(BF16)
        for half in range(2):
            got = jnp.dot(hot, pcodes[:, half * HALF:(half + 1) * HALF], preferred_element_type=F32)
            codes[r, half, rows, :] = got.astype(BF16)
        return carry

    lax.fori_loop(0, 4, pick, 0)

    def rep_of(d, core):
        return ((h + d + 4) % 4) * 2 + core

    def chunk(rep, q):
        return codes.at[rep, :, pl.ds(q * CHUNK, CHUNK), :]

    up, down = (rep_of(1, c), w), (rep_of(-1, c), w)
    twin = (rep_of(0, 1 - c), w)
    for q in range(4):
        send(chunk(r, q), chunk(r, q), zs.at[0, q], zr.at[0, q], up)
        p = (q + 2) % 4
        send(chunk(r, p), chunk(r, p), zs.at[1, p], zr.at[1, p], down)
    for q in range(4):
        send(chunk(r, q), chunk(r, q), ks.at[0, q], kr.at[0, q], twin)

    is_a = r < 4

    def part(j):
        zj, yj, xj = j // 16, (j // 4) % 4, j % 4
        xx, qc = xj // 2, xj % 2
        t = jnp.where(is_a, (yj * 2 + zj) * 2 + xx, (xx * 2 + zj) * 4 + yj)
        return codes.at[r, :, pl.ds(pl.multiple_of(t * PIECE, PIECE), PIECE),
                        pl.ds(pl.multiple_of(qc * 256, 256), 256)]

    def spread(i, carry):
        j = (w + i) % 32
        copy(part(j), a2a.at[w], as_.at[i], ar.at[i], (r, j)).start()
        return carry

    lax.fori_loop(1, 32, spread, 0)
    mine = pltpu.make_async_copy(part(w), a2a.at[w], as_.at[0])
    mine.start()
    mine.wait()

    def collect(i, carry):
        j = (w - i + 32) % 32
        arrived(a2a.at[j], as_.at[i], ar.at[i], (r, j))
        return carry

    lax.fori_loop(1, 32, collect, 0)

    my_k = jnp.where(is_a, y, x)
    my_m = jnp.where(is_a, x, y)
    my_ab = r // 4
    for i in range(8):
        rd = (r + i) % 8
        hd, cd = rd // 2, rd % 2
        owner = rows_ref[hd // 2] * 2 + hd % 2
        got = a2a[owner, cd]
        dst = chosen.at[my_ab, my_k, zl, my_m, r % 4]
        if i == 0:
            dst[...] = got
        else:
            sel[i] = got
            send(sel.at[i], dst, rs.at[i], rr.at[i], (rd, w))
    for i in range(1, 8):
        src = (r - i + 8) % 8
        s_a = src < 4
        dst = chosen.at[src // 4, jnp.where(s_a, y, x), zl, jnp.where(s_a, x, y), src % 4]
        arrived(dst, rs.at[i], rr.at[i], (src, w))

    nothing = lambda *a: None
    gather(chosen, cs, cr, nothing, nothing, nothing)

    def gram(rep, first=False):
        ab, slot = rep // 4, rep % 4
        in_a = ab == 0

        def quarter(qc, carry):
            parts = []
            for t in range(16):
                k = jnp.where(in_a, t // 4, 2 * (t // 8) + qc)
                z = jnp.where(in_a, (t // 2) % 2, (t // 4) % 2)
                m = jnp.where(in_a, 2 * (t % 2) + qc, t % 4)
                parts.append(chosen[ab, k, z, m, slot])
            lhs = jnp.concatenate(parts, axis=0)
            at = pl.ds(pl.multiple_of(qc * 256, 256), 256)
            for half in range(2):
                made = lax.dot_general(lhs, codes[rep, half], (((0,), (0,)), ((), ())),
                                       preferred_element_type=F32)
                cols = slice(half * HALF, (half + 1) * HALF)
                if first:
                    out_ref[at, cols] = made
                else:
                    out_ref[at, cols] += made
            return carry

        lax.fori_loop(0, 2, quarter, 0)

    def twin_arrived(k, q):
        got = chunk(rep_of((0, -1, 1, 2)[k], 1 - c), q)
        arrived(got, ks.at[k, q], kr.at[k, q], twin)

    def to_twin(k, q):
        part_ = chunk(rep_of((0, -1, 1, 2)[k], c), q)
        send(part_, part_, ks.at[k, q], kr.at[k, q], twin)

    gram(r, first=True)
    for q in range(4):
        got = chunk(rep_of(-1, c), q)
        arrived(got, zs.at[0, q], zr.at[0, q], down)
        if q < 2:
            send(got, got, fs.at[0, q], fr.at[0, q], up)
        to_twin(1, q)
        p = (q + 2) % 4
        got = chunk(rep_of(1, c), p)
        arrived(got, zs.at[1, p], zr.at[1, p], up)
        if q < 2:
            send(got, got, fs.at[1, q], fr.at[1, q], down)
        to_twin(2, p)
    for q in range(4):
        twin_arrived(0, q)
    gram(rep_of(0, 1 - c))
    for k, d in ((1, -1), (2, 1)):
        gram(rep_of(d, c))
        for q in range(4):
            twin_arrived(k, q)
        gram(rep_of(d, 1 - c))
    for q in range(2):
        arrived(chunk(rep_of(2, c), q), fs.at[0, q], fr.at[0, q], down)
        to_twin(3, q)
        arrived(chunk(rep_of(2, c), q + 2), fs.at[1, q], fr.at[1, q], up)
        to_twin(3, q + 2)
    gram(rep_of(2, c))
    for q in range(4):
        twin_arrived(3, q)
    gram(rep_of(2, 1 - c))
    out_ref[...] = out_ref[...] * (1.0 / 6144.0)

    for d in sends:
        d.wait_send()

    def sent(i, carry):
        j = (w + i) % 32
        copy(part(j), a2a.at[w], as_.at[i], ar.at[i], (r, j)).wait_send()
        return carry

    lax.fori_loop(1, 32, sent, 0)


def local(pool, ids, block_rows, enc_weight, enc_bias, dec_bias):
    ab, j, wp = (ids % 32) // 16, ids % 16, ids // 32
    zl, y, x = wp // 16, (wp // 4) % 4, wp % 4
    k = jnp.where(ab == 0, y, x)
    m = jnp.where(ab == 0, x, y)
    pos = (ab * 512 + k * 128 + zl * 64 + m * 16 + j).reshape(TOK, 1)
    vmem = pl.BlockSpec(memory_space=pltpu.VMEM)
    smem = pl.BlockSpec(memory_space=pltpu.SMEM)
    dma = pltpu.SemaphoreType.DMA
    return pl.pallas_call(
        kernel,
        out_shape=jax.ShapeDtypeStruct((ROWS, PANEL), F32),
        in_specs=[vmem, vmem, smem, pl.BlockSpec(memory_space=pl.ANY), vmem, vmem],
        out_specs=vmem,
        scratch_shapes=[
            pltpu.VMEM((D, PANEL), BF16),
            pltpu.VMEM((2, 4, 2, 4, 16, D), BF16),
            pltpu.VMEM((1024, PANEL), BF16),
            pltpu.VMEM((8, 2, TOK, HALF), BF16),
            pltpu.VMEM((32, 2, PIECE, 256), BF16),
            pltpu.VMEM((8, PIECE, 256), BF16),
            pltpu.VMEM((2, 4, 2, 4, 4, PIECE, 256), BF16),
            dma,
            dma((2, 13)), dma((2, 13)),
            dma((2, 13)), dma((2, 13)),
            dma((32,)), dma((32,)),
            dma((8,)), dma((8,)),
            dma((2, 4)), dma((2, 4)),
            dma((2, 2)), dma((2, 2)),
            dma((4, 4)), dma((4, 4)),
        ],
        compiler_params=pltpu.CompilerParams(
            collective_id=0, has_side_effects=True, vmem_limit_bytes=58 * 1024 * 1024),
    )(pool, pos, block_rows, enc_weight, enc_bias.reshape(1, PANEL), dec_bias.reshape(1, D))


def solution(mesh):
    placed = (P(("rep", "wide"), None), P("rep"), P(), P(None, "wide"), P("wide"), P())
    return jax.shard_map(
        local, mesh=mesh, in_specs=placed, out_specs=P("rep", "wide"), check_vma=False
    )
```

time: 765 us -> 251 us (0.33)
  waiting for transfers between devices: 694 us -> 0 us
  Pallas kernels: 0 us -> 243 us
  matrix products: 27.9 us -> 0 us
  between operations: 14.6 us -> 0.01 us
  local copies, waits for them, and re-layouts: 17.8 us -> 4.07 us
  other arithmetic: 9.4 us -> 0.72 us
    psum x1 -> x0, waiting for transfers between devices: 340 us -> none  [from_root(): return lax.psum(kept, axis)]
    pallas_call x0 -> x1, Pallas kernels: none -> 243 us  [local(): pl.pallas_call(kernel, out_shape=jax.ShapeDtypeStruct((ROWS, PANEL), F32)...]
    reduce_scatter x1 -> x0, waiting for transfers between devices: 183 us -> none  [local(): summed = lax.psum_scatter(panel_sum, 'rep', scatter_dimension=0, tiled=True)]
    all_gather x1 -> x0, waiting for transfers between devices: 171 us -> none  [local(): table = lax.all_gather(pool, 'wide', axis=0, tiled=True)]
    dot_general x2 -> x0, matrix products: 27.9 us -> none  [the longest x1 15.3 us: local(): lax.dot_general(chosen, codes, (((0,), (0,)), ((), ())), preferred_elemen...]
    gather x1 -> x0, local copies, waits for them, and re-layouts: 16.4 us -> none  [local(): residual = jnp.take(table, ids, axis=0)]
  transfers between devices with their start and end apart: 3 -> 0, of which waited for: 3 -> 0; matrix products, arithmetic and copies ran while one was open for 0% -> 0% of each run, Pallas kernels for 0% -> 0%
where the time goes in v1:
time: 251 us; the launch traced here: 248 us
  Pallas kernels  243 us (97%)
  local copies, waits for them, and re-layouts  4.07 us (2%)
    pallas_call x1, Pallas kernels, local(): pl.pallas_call(kernel, out_shape=jax.ShapeDtypeStruct((ROWS, PANEL), F32)...  243 us

profile of v1, /device:TPU:2, one launch (start us, length us, event | category | flops | bytes accessed | tf_op | source)
XLA Modules:
  0.0 247.5 jit_solution(7063880465380137060)
XLA Ops:
  0.0 0.7 fusion.6
  0.7 0.9 reshape.12.pos_ref
  1.6 242.7 %shard_map.64 = f32[512,1024]{1,0:T(8,128)} custom-call(bf16[32,4096]{1,0:T(8,128)(2,1)} %pool_ref.1, s32[768,1]{1,0:T(8,128)} %reshape.12.pos_ref, s32[2]{0:T(128)} %rows_ref.1, bf16[4096,1024]{1,0:T(8,128)(2,1)} %w_hbm.1, f32[1,1024]{1,0:T(1,128)} %bitcast.3, f32[1,4096]{1,0:T(1,128)} %bitcast.2), custom_call_target="tpu_custom_call" | custom-call | tf_op jit(solution)/shard_map/pallas_call | solution.py:324
  244.4 3.2 %copy.9 = f32[512,1024]{1,0:T(8,128)} copy(f32[512,1024]{1,0:T(8,128)} %shard_map.64) | data formatting | bytes 4194304

commit v2 on v0

v2 whole, which is shorter than its diff:
```python
import functools

import jax
import jax.numpy as jnp
from jax import lax
from jax.experimental import pallas as pl
from jax.experimental.pallas import tpu as pltpu
from jax.sharding import PartitionSpec as P

BLOCK = 2048
D = 4096
TOK = 768
PANEL = 1024
HALF = 512
ROWS = 512
PIECE = 48
CHUNK = 192
MESH = pl.DeviceIdType.MESH
F32 = jnp.float32
BF16 = jnp.bfloat16


def kernel(pool_ref, pos_ref, rows_ref, w_hbm, eb_ref, db_ref, out_ref,
           w_vm, cent, pcodes, codes, ybuf, xsend, xbuf, zsend, zbuf, sel, chosen,
           w_sem, go, l_sem, ps, pr, cs, cr, ys, yr, xs, xr, qs, qr, rs, rr, zs, zr, fs, fr, ks, kr):
    r = lax.axis_index("rep")
    w = lax.axis_index("wide")
    h, core = r // 2, r % 2
    zl, y, x = w // 16, (w // 4) % 4, w % 4

    def wide_of(zz, yy, xx):
        return zz * 16 + yy * 4 + xx

    w_copy = pltpu.make_async_copy(w_hbm, w_vm, w_sem)
    w_copy.start()

    barrier = pltpu.get_barrier_semaphore()
    partners = [((r + i) % 8, w) for i in range(1, 8)]
    partners += [(r, wide_of(zl, (y + i) % 4, x)) for i in range(1, 4)]
    partners += [(r, wide_of(zl, y, (x + i) % 4)) for i in range(1, 4)]
    partners += [((r + i) % 8, wide_of(1 - zl, y, x)) for i in range(8)]
    for device in partners:
        pl.semaphore_signal(barrier, inc=1, device_id=device, device_id_type=MESH)

    for ab in range(2):
        values = pool_ref[ab * 16:(ab + 1) * 16, :].astype(F32)
        power = jnp.mean(values * values, axis=-1, keepdims=True)
        centered = (values * lax.rsqrt(power + 1e-06) - db_ref[...]).astype(BF16)
        if ab == 0:
            cent[0, y, zl, x] = centered
        else:
            cent[1, x, zl, y] = centered

    pl.semaphore_wait(barrier, len(partners))

    def program(c):
        sends = []
        twin = (h * 2 + 1 - c, w)
        other = (r, wide_of(1 - zl, y, x))

        def copy(src, dst, ssem, rsem, dev):
            return pltpu.make_async_remote_copy(
                src_ref=src, dst_ref=dst, send_sem=ssem, recv_sem=rsem,
                device_id=dev, device_id_type=MESH)

        def send(src, dst, ssem, rsem, dev):
            d = copy(src, dst, ssem, rsem, dev)
            d.start()
            sends.append(d)

        def arrived(dst, ssem, rsem, dev):
            copy(dst, dst, ssem, rsem, dev).wait_recv()

        place = ((y, x), (x, y))
        steps = (1, -1)

        def first(ab, d):
            if ab == 0:
                return (r, wide_of(zl, y, (x + d + 4) % 4))
            return (r, wide_of(zl, (y + d + 4) % 4, x))

        def second(ab, d):
            return first(1 - ab, d)

        def gather_rows(hold):
            def piece(ab, dk, e, dm):
                k, m = place[ab]
                return cent.at[ab, (k + dk + 4) % 4, zl if e == 0 else 1 - zl, (m + dm + 4) % 4]

            def got(ab, at, s, dev):
                arrived(at, ps.at[ab, s], pr.at[ab, s], dev)

            def put(ab, at, s, dev):
                send(at, at, ps.at[ab, s], pr.at[ab, s], dev)

            held = []

            def across(ab, e, dm):
                def go_across():
                    for i, d in enumerate(steps):
                        put(ab, piece(ab, 0, e, dm), 7 + i * 8 + e * 4 + dm % 4, second(ab, d))
                held.append(go_across)
                if hold is None:
                    held.pop()()

            for ab in range(2):
                put(ab, piece(ab, 0, 0, 0), 0, other)
                for i, d in enumerate(steps):
                    put(ab, piece(ab, 0, 0, 0), 1 + i * 2, first(ab, d))
                across(ab, 0, 0)
            for ab in range(2):
                got(ab, piece(ab, 0, 1, 0), 0, other)
                for i, d in enumerate(steps):
                    put(ab, piece(ab, 0, 1, 0), 2 + i * 2, first(ab, d))
                across(ab, 1, 0)
            for e in range(2):
                for i, d in ((0, 1), (1, -1)):
                    for ab in range(2):
                        got(ab, piece(ab, 0, e, -d), 1 + i * 2 + e, first(ab, -d))
                        if e == i:
                            put(ab, piece(ab, 0, e, -d), 5 + i, first(ab, d))
                        across(ab, e, -d)
            for i, d in enumerate(steps):
                for ab in range(2):
                    got(ab, piece(ab, 0, i, 2), 5 + i, first(ab, -d))
                    across(ab, i, 2)
            if hold is not None:
                hold()
                for task in held:
                    task()
            yield 3
            order = (0, -1, 1, 2)
            for dm in order:
                for ab in range(2):
                    for i, d in enumerate(steps):
                        s = 7 + i * 8 + i * 4 + dm % 4
                        got(ab, piece(ab, -d, i, dm), s, second(ab, -d))
                        put(ab, piece(ab, -d, i, dm), 23 + i * 4 + dm % 4, second(ab, d))
            for i, d in enumerate(steps):
                for ab in range(2):
                    for dm in order:
                        got(ab, piece(ab, -d, 1 - i, dm), 7 + i * 8 + (1 - i) * 4 + dm % 4, second(ab, -d))
                yield 5 + i
            for ab in range(2):
                for i, d in enumerate(steps):
                    for dm in order:
                        got(ab, piece(ab, 2, i, dm), 23 + i * 4 + dm % 4, second(ab, -d))
            yield 7

        def gather_chosen(par):
            ss, sr = cs.at[par], cr.at[par]

            def move(ab, at, s, dev):
                send(at, at, ss.at[ab, s], sr.at[ab, s], dev)

            def got(ab, at, s, dev):
                arrived(at, ss.at[ab, s], sr.at[ab, s], dev)

            for ab in range(2):
                k, m = place[ab]
                for i, d in enumerate(steps):
                    move(ab, chosen.at[par, ab, k, m], i, first(ab, d))
            yield 0
            for ab in range(2):
                k, m = place[ab]
                for i, d in enumerate(steps):
                    at = chosen.at[par, ab, k, (m - d + 4) % 4]
                    got(ab, at, i, first(ab, -d))
                    move(ab, chosen.at[par, ab, k, (m - d + 4) % 4, i], 2 + i, first(ab, d))
            yield 1
            for ab in range(2):
                k, m = place[ab]
                for i, d in enumerate(steps):
                    got(ab, chosen.at[par, ab, k, (m + 2) % 4, i], 2 + i, first(ab, -d))
                for i, d in enumerate(steps):
                    move(ab, chosen.at[par, ab, k], 4 + i, second(ab, d))
            yield 2
            for ab in range(2):
                k, m = place[ab]
                for i, d in enumerate(steps):
                    kk = (k - d + 4) % 4
                    got(ab, chosen.at[par, ab, kk], 4 + i, second(ab, -d))
                    move(ab, chosen.at[par, ab, kk, pl.ds(2 * i, 2)], 6 + i, second(ab, d))
            yield 3
            for ab in range(2):
                k, m = place[ab]
                for i, d in enumerate(steps):
                    got(ab, chosen.at[par, ab, (k + 2) % 4, pl.ds(2 * i, 2)], 6 + i, second(ab, -d))
            yield 4

        def until(task, mark):
            while next(task) != mark:
                pass

        def encode(d):
            ky, kx = (y + d + 4) % 4, (x + d + 4) % 4

            def tile(n, carry):
                cols = pl.ds(pl.multiple_of(n * 256, 256), 256)
                lhs = jnp.concatenate(
                    [cent[0, ky].reshape(128, D), cent[1, kx].reshape(128, D)], axis=0)
                before = jnp.dot(lhs, w_vm[:, cols], preferred_element_type=F32) + eb_ref[:, cols]
                made = jnp.maximum(before, 0.0).astype(BF16)
                pcodes[pl.ds(pl.multiple_of(ky * 128, 128), 128), cols] = made[:128]
                pcodes[pl.ds(pl.multiple_of(512 + kx * 128, 128), 128), cols] = made[128:]
                return carry

            lax.fori_loop(0, 4, tile, 0)

        rows = gather_rows(None if c == 0 else lambda: pl.semaphore_wait(go, 1))
        until(rows, 3)
        w_copy.wait()
        encode(0)
        until(rows, 5)
        encode(-1)
        until(rows, 6)
        encode(1)
        until(rows, 7)
        if c == 0:
            pl.semaphore_signal(go, inc=1, device_id=twin, device_id_type=MESH)
        encode(2)

        def pick(q, carry):
            at = pl.ds(pl.multiple_of(q * CHUNK, CHUNK), CHUNK)
            hot = (pos_ref[at, :] == lax.broadcasted_iota(jnp.int32, (CHUNK, 1024), 1)).astype(BF16)
            for half in range(2):
                got = jnp.dot(hot, pcodes[:, half * HALF:(half + 1) * HALF], preferred_element_type=F32)
                codes[r, half, at, :] = got.astype(BF16)
            return carry

        lax.fori_loop(0, 4, pick, 0)

        def rep_of(d, core_):
            return ((h + d + 4) % 4) * 2 + core_

        def chunk(rep, q):
            return codes.at[rep, :, pl.ds(q * CHUNK, CHUNK), :]

        up, down = (rep_of(1, c), w), (rep_of(-1, c), w)

        def along_z(q):
            send(chunk(r, q), chunk(r, q), zs.at[0, q], zr.at[0, q], up)
            p = (q + 2) % 4
            send(chunk(r, p), chunk(r, p), zs.at[1, p], zr.at[1, p], down)

        def to_twin(k, q):
            part = chunk(rep_of((0, -1, 1, 2)[k], c), q)
            send(part, part, ks.at[k, q], kr.at[k, q], twin)

        def twin_arrived(k):
            for q in range(4):
                arrived(chunk(rep_of((0, -1, 1, 2)[k], 1 - c), q), ks.at[k, q], kr.at[k, q], twin)

        def pass_on(q):
            got = chunk(rep_of(-1, c), q)
            arrived(got, zs.at[0, q], zr.at[0, q], down)
            if q < 2:
                send(got, got, fs.at[0, q], fr.at[0, q], up)
            to_twin(1, q)
            p = (q + 2) % 4
            got = chunk(rep_of(1, c), p)
            arrived(got, zs.at[1, p], zr.at[1, p], up)
            if q < 2:
                send(got, got, fs.at[1, q], fr.at[1, q], down)
            to_twin(2, p)

        def far_codes():
            for q in range(2):
                arrived(chunk(rep_of(2, c), q), fs.at[0, q], fr.at[0, q], down)
                to_twin(3, q)
                arrived(chunk(rep_of(2, c), q + 2), fs.at[1, q], fr.at[1, q], up)
                to_twin(3, q + 2)

        def owner(k, p):
            return rows_ref[k] * 2 + p

        def route():
            for i in range(1, 4):
                yy = (y + i) % 4
                part = codes.at[r, :, pl.ds(pl.multiple_of(yy * CHUNK, CHUNK), CHUNK), :]
                send(part, ybuf.at[y], ys.at[i], yr.at[i], (r, wide_of(zl, yy, x)))
            mine = pltpu.make_async_copy(
                codes.at[r, :, pl.ds(pl.multiple_of(y * CHUNK, CHUNK), CHUNK), :], ybuf.at[y], l_sem)
            mine.start()
            yield 0
            mine.wait()
            for i in range(1, 4):
                src = (y - i + 4) % 4
                arrived(ybuf.at[src], ys.at[i], yr.at[i], (r, wide_of(zl, src, x)))
            for k in range(2):
                xsend[k] = ybuf[(owner(k, x % 2) // 4) % 4]
            for i in range(1, 4):
                xx = (x + i) % 4
                part = xsend.at[:, :, pl.ds(pl.multiple_of(xx * PIECE, PIECE), PIECE), :]
                send(part, xbuf.at[x], xs.at[i], xr.at[i], (r, wide_of(zl, y, xx)))
            xbuf[x] = xsend[:, :, pl.ds(pl.multiple_of(x * PIECE, PIECE), PIECE), :]
            yield 1
            for i in range(1, 4):
                src = (x - i + 4) % 4
                arrived(xbuf.at[src], xs.at[i], xr.at[i], (r, wide_of(zl, y, src)))
            for hd in range(4):
                k, p = hd // 2, hd % 2
                xo = owner(k, p) % 4
                zsend[hd] = xbuf[xo, k, :, :, pl.ds(pl.multiple_of((1 - zl) * 256, 256), 256)]
                zbuf[zl, hd] = xbuf[xo, k, :, :, pl.ds(pl.multiple_of(zl * 256, 256), 256)]
            send(zsend, zbuf.at[zl], qs, qr, other)
            yield 2
            arrived(zbuf.at[1 - zl], qs, qr, other)
            ab = h // 2
            place_k = jnp.where(ab == 0, y, x)
            place_m = jnp.where(ab == 0, x, y)
            dst = chosen.at[c, ab, place_k, place_m, zl, h % 2]
            for i in (4, 3, 5, 2, 6, 1, 7, 0):
                rd = (r + i) % 8
                hd, cd = rd // 2, (c + i) % 2
                sel[i] = zbuf[owner(hd // 2, hd % 2) // 16, hd, cd]
                if i == 0:
                    dst[...] = sel[i]
                else:
                    send(sel.at[i], dst, rs.at[0, i], rr.at[0, i], (rd, w))
                send(sel.at[i], dst, rs.at[1, i], rr.at[1, i], (rd, other[1]))
            yield 3

        def pieces_arrived(par):
            for i in range(8):
                if (c - i) % 2 != par:
                    continue
                src = (r - i + 8) % 8
                hs = src // 2
                ab = hs // 2
                at = (par, ab, jnp.where(ab == 0, y, x), jnp.where(ab == 0, x, y))
                if i > 0:
                    arrived(chosen.at[at + (zl, hs % 2)], rs.at[0, i], rr.at[0, i], (src, w))
                arrived(chosen.at[at + (1 - zl, hs % 2)], rs.at[1, i], rr.at[1, i], (src, other[1]))

        def gram(d, par, first=False):
            hs = (h + d + 4) % 4
            ab, slot = hs // 2, hs % 2
            rep = hs * 2 + par

            def quarter(qc, carry):
                parts = []
                for t in range(16):
                    k = jnp.where(ab == 0, t // 4, t % 4)
                    m = jnp.where(ab == 0, t % 4, t // 4)
                    parts.append(chosen[par, ab, k, m, qc, slot])
                lhs = jnp.concatenate(parts, axis=0)
                at = pl.ds(pl.multiple_of(qc * 256, 256), 256)
                for half in range(2):
                    made = lax.dot_general(lhs, codes[rep, half], (((0,), (0,)), ((), ())),
                                           preferred_element_type=F32)
                    cols = slice(half * HALF, (half + 1) * HALF)
                    if first:
                        out_ref[at, cols] = made
                    else:
                        out_ref[at, cols] += made
                return carry

            lax.fori_loop(0, 2, quarter, 0)

        deal = route()
        spread = [gather_chosen(par) for par in range(2)]
        until(deal, 0)
        if c == 0:
            along_z(0)
            along_z(1)
            along_z(2)
            for q in range(4):
                to_twin(0, q)
            until(deal, 1)
            until(deal, 2)
            until(deal, 3)
            along_z(3)
            pass_on(0)
            pass_on(1)
            pieces_arrived(0)
            until(spread[0], 2)
            pass_on(2)
            pass_on(3)
            until(spread[0], 4)
            gram(0, 0, first=True)
            gram(-1, 0)
            gram(1, 0)
            pieces_arrived(1)
            until(spread[1], 2)
            far_codes()
            until(spread[1], 4)
            gram(2, 0)
            for k, d in enumerate((0, -1, 1, 2)):
                twin_arrived(k)
                gram(d, 1)
        else:
            along_z(0)
            along_z(1)
            for q in range(4):
                to_twin(0, q)
            pieces_arrived(0)
            until(spread[0], 1)
            until(deal, 1)
            until(spread[0], 2)
            until(deal, 2)
            until(deal, 3)
            along_z(2)
            along_z(3)
            pass_on(0)
            pass_on(1)
            until(spread[0], 4)
            pieces_arrived(1)
            until(spread[1], 2)
            pass_on(2)
            pass_on(3)
            until(spread[1], 4)
            twin_arrived(0)
            gram(0, 0, first=True)
            gram(0, 1)
            for k, d in ((1, -1), (2, 1)):
                twin_arrived(k)
                gram(d, 0)
                gram(d, 1)
            twin_arrived(3)
            gram(2, 0)
            far_codes()
            gram(2, 1)

        for d in sends:
            d.wait_send()

    @pl.when(core == 0)
    def _():
        program(0)

    @pl.when(core == 1)
    def _():
        program(1)


def local(pool, ids, block_rows, enc_weight, enc_bias, dec_bias):
    ab, j, wp = (ids % 32) // 16, ids % 16, ids // 32
    zl, y, x = wp // 16, (wp // 4) % 4, wp % 4
    k = jnp.where(ab == 0, y, x)
    m = jnp.where(ab == 0, x, y)
    pos = (ab * 512 + k * 128 + zl * 64 + m * 16 + j).reshape(TOK, 1)
    vmem = pl.BlockSpec(memory_space=pltpu.VMEM)
    smem = pl.BlockSpec(memory_space=pltpu.SMEM)
    dma = pltpu.SemaphoreType.DMA
    summed = pl.pallas_call(
        kernel,
        out_shape=jax.ShapeDtypeStruct((ROWS, PANEL), F32),
        in_specs=[vmem, vmem, smem, pl.BlockSpec(memory_space=pl.ANY), vmem, vmem],
        out_specs=vmem,
        scratch_shapes=[
            pltpu.VMEM((D, PANEL), BF16),
            pltpu.VMEM((2, 4, 2, 4, 16, D), BF16),
            pltpu.VMEM((1024, PANEL), BF16),
            pltpu.VMEM((8, 2, TOK, HALF), BF16),
            pltpu.VMEM((4, 2, CHUNK, HALF), BF16),
            pltpu.VMEM((2, 2, CHUNK, HALF), BF16),
            pltpu.VMEM((4, 2, 2, PIECE, HALF), BF16),
            pltpu.VMEM((4, 2, PIECE, 256), BF16),
            pltpu.VMEM((2, 4, 2, PIECE, 256), BF16),
            pltpu.VMEM((8, PIECE, 256), BF16),
            pltpu.VMEM((2, 2, 4, 4, 2, 2, PIECE, 256), BF16),
            dma, pltpu.SemaphoreType.REGULAR, dma,
            dma((2, 31)), dma((2, 31)),
            dma((2, 2, 8)), dma((2, 2, 8)),
            dma((4,)), dma((4,)),
            dma((4,)), dma((4,)),
            dma, dma,
            dma((2, 8)), dma((2, 8)),
            dma((2, 4)), dma((2, 4)),
            dma((2, 2)), dma((2, 2)),
            dma((4, 4)), dma((4, 4)),
        ],
        compiler_params=pltpu.CompilerParams(
            collective_id=0, has_side_effects=True, vmem_limit_bytes=58 * 1024 * 1024),
    )(pool, pos, block_rows, enc_weight, enc_bias.reshape(1, PANEL), dec_bias.reshape(1, D))
    return summed * (1.0 / 6144.0)


def solution(mesh):
    placed = (P(("rep", "wide"), None), P("rep"), P(), P(None, "wide"), P("wide"), P())
    return jax.shard_map(
        local, mesh=mesh, in_specs=placed, out_specs=P("rep", "wide"), check_vma=False
    )
```

time: 765 us -> 189 us (0.25)
  waiting for transfers between devices: 694 us -> 0 us
  Pallas kernels: 0 us -> 183 us
  matrix products: 27.9 us -> 0 us
  local copies, waits for them, and re-layouts: 17.8 us -> 0.92 us
  between operations: 14.6 us -> 0.01 us
    psum x1 -> x0, waiting for transfers between devices: 340 us -> none  [from_root(): return lax.psum(kept, axis)]
    pallas_call x0 -> x1, Pallas kernels: none -> 183 us  [local(): pl.pallas_call(kernel, out_shape=jax.ShapeDtypeStruct((ROWS, PANEL), F32)...]
    reduce_scatter x1 -> x0, waiting for transfers between devices: 183 us -> none  [local(): summed = lax.psum_scatter(panel_sum, 'rep', scatter_dimension=0, tiled=True)]
    all_gather x1 -> x0, waiting for transfers between devices: 171 us -> none  [local(): table = lax.all_gather(pool, 'wide', axis=0, tiled=True)]
    dot_general x2 -> x0, matrix products: 27.9 us -> none  [the longest x1 15.3 us: local(): lax.dot_general(chosen, codes, (((0,), (0,)), ((), ())), preferred_elemen...]
    gather x1 -> x0, local copies, waits for them, and re-layouts: 16.4 us -> none  [local(): residual = jnp.take(table, ids, axis=0)]
  transfers between devices with their start and end apart: 3 -> 0, of which waited for: 3 -> 0; matrix products, arithmetic and copies ran while one was open for 0% -> 0% of each run, Pallas kernels for 0% -> 0%
where the time goes in v2:
time: 189 us; the launch traced here: 188 us
  Pallas kernels  183 us (97%)
  other arithmetic  4.01 us (2%)
    pallas_call x1, Pallas kernels, local(): pl.pallas_call(kernel, out_shape=jax.ShapeDtypeStruct((ROWS, PANEL), F32)...  183 us

profile of v2, /device:TPU:2, one launch (start us, length us, event | category | flops | bytes accessed | tf_op | source)
XLA Modules:
  0.0 188.1 jit_solution(10512095676457021531)
XLA Ops:
  0.0 0.7 fusion.6
  0.7 0.9 reshape.12.pos_ref
  1.6 183.2 %shard_map.64 = f32[512,1024]{1,0:T(8,128)} custom-call(bf16[32,4096]{1,0:T(8,128)(2,1)} %pool_ref.1, s32[768,1]{1,0:T(8,128)} %reshape.12.pos_ref, s32[2]{0:T(128)} %rows_ref.1, bf16[4096,1024]{1,0:T(8,128)(2,1)} %w_hbm.1, f32[1,1024]{1,0:T(1,128)} %bitcast.3, f32[1,4096]{1,0:T(1,128)} %bitcast.2), custom_call_target="tpu_custom_call" | custom-call | tf_op jit(solution)/shard_map/pallas_call | solution.py:446
  184.8 3.3 %broadcast_multiply_fusion = f32[512,1024]{1,0:T(8,128)} fusion(f32[512,1024]{1,0:T(8,128)} %shard_map.64), kind=kLoop, calls=%fused_computation | loop fusion | flops 524288 | bytes 4194304 | tf_op jit(solution)/shard_map/mul | solution.py:477

commit v3 on v2

--- a/solution.py
+++ b/solution.py
@@ -1,5 +1,3 @@
-import functools
-
 import jax
 import jax.numpy as jnp
 from jax import lax
@@ -20,8 +18,8 @@
 BF16 = jnp.bfloat16
 
 
-def kernel(pool_ref, pos_ref, rows_ref, w_hbm, eb_ref, db_ref, out_ref,
-           w_vm, cent, pcodes, codes, ybuf, xsend, xbuf, zsend, zbuf, sel, chosen,
+def kernel(pool_ref, ids_ref, rows_ref, w_hbm, eb_ref, db_ref, out_ref,
+           pos_ref, w_vm, cent, pcodes, codes, ybuf, xsend, xbuf, zsend, zbuf, sel, chosen,
            w_sem, go, l_sem, ps, pr, cs, cr, ys, yr, xs, xr, qs, qr, rs, rr, zs, zr, fs, fr, ks, kr):
     r = lax.axis_index("rep")
     w = lax.axis_index("wide")
@@ -51,6 +49,15 @@
         else:
             cent[1, x, zl, y] = centered
 
+    for n in range(TOK // 128):
+        ids = ids_ref[n * 128:(n + 1) * 128].reshape(1, 128)
+        ab, wp = (ids // 16) % 2, ids // 32
+        z_, y_, x_ = wp // 16, (wp // 4) % 4, wp % 4
+        k_ = jnp.where(ab == 0, y_, x_)
+        m_ = jnp.where(ab == 0, x_, y_)
+        place = ab * 512 + k_ * 128 + z_ * 64 + m_ * 16 + ids % 16
+        pos_ref[n * 128:(n + 1) * 128, :] = jnp.broadcast_to(place, (128, 128)).T
+
     pl.semaphore_wait(barrier, len(partners))
 
     def program(c):
@@ -93,15 +100,12 @@
             def put(ab, at, s, dev):
                 send(at, at, ps.at[ab, s], pr.at[ab, s], dev)
 
-            held = []
+            if hold is not None:
+                hold()
 
             def across(ab, e, dm):
-                def go_across():
-                    for i, d in enumerate(steps):
-                        put(ab, piece(ab, 0, e, dm), 7 + i * 8 + e * 4 + dm % 4, second(ab, d))
-                held.append(go_across)
-                if hold is None:
-                    held.pop()()
+                for i, d in enumerate(steps):
+                    put(ab, piece(ab, 0, e, dm), 7 + i * 8 + e * 4 + dm % 4, second(ab, d))
 
             for ab in range(2):
                 put(ab, piece(ab, 0, 0, 0), 0, other)
@@ -124,10 +128,6 @@
                 for ab in range(2):
                     got(ab, piece(ab, 0, i, 2), 5 + i, first(ab, -d))
                     across(ab, i, 2)
-            if hold is not None:
-                hold()
-                for task in held:
-                    task()
             yield 3
             order = (0, -1, 1, 2)
             for dm in order:
@@ -220,28 +220,34 @@
             pl.semaphore_signal(go, inc=1, device_id=twin, device_id_type=MESH)
         encode(2)
 
-        def pick(q, carry):
+        def rep_of(d, core_):
+            return ((h + d + 4) % 4) * 2 + core_
+
+        def chunk(rep, q):
+            return codes.at[rep, :, pl.ds(q * CHUNK, CHUNK), :]
+
+        up, down = (rep_of(1, c), w), (rep_of(-1, c), w)
+
+        def along_z(q):
+            send(chunk(r, q), chunk(r, q), zs.at[0, q], zr.at[0, q], up)
+            p = (q + 2) % 4
+            send(chunk(r, p), chunk(r, p), zs.at[1, p], zr.at[1, p], down)
+
+        def pick(i, carry):
+            q = (i % 2) * 2 + i // 2
             at = pl.ds(pl.multiple_of(q * CHUNK, CHUNK), CHUNK)
-            hot = (pos_ref[at, :] == lax.broadcasted_iota(jnp.int32, (CHUNK, 1024), 1)).astype(BF16)
+            place_of = pos_ref[at, :]
+            lane = lax.broadcasted_iota(jnp.int32, (CHUNK, 128), 1)
+            hot = jnp.concatenate(
+                [(place_of == lane + 128 * n).astype(F32) for n in range(8)], axis=1).astype(BF16)
             for half in range(2):
                 got = jnp.dot(hot, pcodes[:, half * HALF:(half + 1) * HALF], preferred_element_type=F32)
                 codes[r, half, at, :] = got.astype(BF16)
             return carry
 
-        lax.fori_loop(0, 4, pick, 0)
-
-        def rep_of(d, core_):
-            return ((h + d + 4) % 4) * 2 + core_
-
-        def chunk(rep, q):
-            return codes.at[rep, :, pl.ds(q * CHUNK, CHUNK), :]
-
-        up, down = (rep_of(1, c), w), (rep_of(-1, c), w)
-
-        def along_z(q):
-            send(chunk(r, q), chunk(r, q), zs.at[0, q], zr.at[0, q], up)
-            p = (q + 2) % 4
-            send(chunk(r, p), chunk(r, p), zs.at[1, p], zr.at[1, p], down)
+        lax.fori_loop(0, 2, pick, 0)
+        along_z(0)
+        lax.fori_loop(2, 4, pick, 0)
 
         def to_twin(k, q):
             part = chunk(rep_of((0, -1, 1, 2)[k], c), q)
@@ -360,17 +366,16 @@
 
         deal = route()
         spread = [gather_chosen(par) for par in range(2)]
-        until(deal, 0)
         if c == 0:
-            along_z(0)
+            until(deal, 0)
             along_z(1)
             along_z(2)
+            along_z(3)
             for q in range(4):
                 to_twin(0, q)
             until(deal, 1)
             until(deal, 2)
             until(deal, 3)
-            along_z(3)
             pass_on(0)
             pass_on(1)
             pieces_arrived(0)
@@ -384,19 +389,20 @@
             pieces_arrived(1)
             until(spread[1], 2)
             far_codes()
+            until(spread[1], 3)
+            gram(2, 0)
             until(spread[1], 4)
-            gram(2, 0)
             for k, d in enumerate((0, -1, 1, 2)):
                 twin_arrived(k)
                 gram(d, 1)
         else:
-            along_z(0)
-            along_z(1)
+            until(deal, 0)
             for q in range(4):
                 to_twin(0, q)
             pieces_arrived(0)
             until(spread[0], 1)
             until(deal, 1)
+            along_z(1)
             until(spread[0], 2)
             until(deal, 2)
             until(deal, 3)
@@ -405,18 +411,21 @@
             pass_on(0)
             pass_on(1)
             until(spread[0], 4)
+            twin_arrived(0)
+            gram(0, 0, first=True)
             pieces_arrived(1)
             until(spread[1], 2)
             pass_on(2)
+            until(spread[1], 3)
             pass_on(3)
+            twin_arrived(1)
+            gram(-1, 0)
             until(spread[1], 4)
-            twin_arrived(0)
-            gram(0, 0, first=True)
             gram(0, 1)
-            for k, d in ((1, -1), (2, 1)):
-                twin_arrived(k)
-                gram(d, 0)
-                gram(d, 1)
+            gram(-1, 1)
+            twin_arrived(2)
+            gram(1, 0)
+            gram(1, 1)
             twin_arrived(3)
             gram(2, 0)
             far_codes()
@@ -435,11 +444,6 @@
 
 
 def local(pool, ids, block_rows, enc_weight, enc_bias, dec_bias):
-    ab, j, wp = (ids % 32) // 16, ids % 16, ids // 32
-    zl, y, x = wp // 16, (wp // 4) % 4, wp % 4
-    k = jnp.where(ab == 0, y, x)
-    m = jnp.where(ab == 0, x, y)
-    pos = (ab * 512 + k * 128 + zl * 64 + m * 16 + j).reshape(TOK, 1)
     vmem = pl.BlockSpec(memory_space=pltpu.VMEM)
     smem = pl.BlockSpec(memory_space=pltpu.SMEM)
     dma = pltpu.SemaphoreType.DMA
@@ -449,6 +453,7 @@
         in_specs=[vmem, vmem, smem, pl.BlockSpec(memory_space=pl.ANY), vmem, vmem],
         out_specs=vmem,
         scratch_shapes=[
+            pltpu.VMEM((TOK, 128), jnp.int32),
             pltpu.VMEM((D, PANEL), BF16),
             pltpu.VMEM((2, 4, 2, 4, 16, D), BF16),
             pltpu.VMEM((1024, PANEL), BF16),
@@ -473,7 +478,7 @@
         ],
         compiler_params=pltpu.CompilerParams(
             collective_id=0, has_side_effects=True, vmem_limit_bytes=58 * 1024 * 1024),
-    )(pool, pos, block_rows, enc_weight, enc_bias.reshape(1, PANEL), dec_bias.reshape(1, D))
+    )(pool, ids, block_rows, enc_weight, enc_bias.reshape(1, PANEL), dec_bias.reshape(1, D))
     return summed * (1.0 / 6144.0)
 
 

time: 189 us -> 173 us (0.915)
  Pallas kernels: 183 us -> 169 us
    pallas_call x1, Pallas kernels: 183 us -> 169 us  [local(): pl.pallas_call(kernel, out_shape=jax.ShapeDtypeStruct((ROWS, PANEL), F32)...]
where the time goes in v3:
time: 173 us; the launch traced here: 172 us
  Pallas kernels  169 us (98%)
  other arithmetic  3.29 us (2%)
    pallas_call x1, Pallas kernels, local(): pl.pallas_call(kernel, out_shape=jax.ShapeDtypeStruct((ROWS, PANEL), F32)...  169 us

profile of v3, /device:TPU:2, one launch (start us, length us, event | category | flops | bytes accessed | tf_op | source)
XLA Modules:
  0.0 172.1 jit_solution(17681530873646904621)
XLA Ops:
  0.0 168.8 %shard_map.64 = f32[512,1024]{1,0:T(8,128)} custom-call(bf16[32,4096]{1,0:T(8,128)(2,1)} %pool_ref.1, s32[768]{0:T(1024)} %ids_ref.1, s32[2]{0:T(128)} %rows_ref.1, bf16[4096,1024]{1,0:T(8,128)(2,1)} %w_hbm.1, f32[1,1024]{1,0:T(1,128)} %bitcast.3, f32[1,4096]{1,0:T(1,128)} %bitcast.2), custom_call_target="tpu_custom_call" | custom-call | tf_op jit(solution)/shard_map/pallas_call | solution.py:450
  168.8 3.3 %broadcast_multiply_fusion = f32[512,1024]{1,0:T(8,128)} fusion(f32[512,1024]{1,0:T(8,128)} %shard_map.64), kind=kLoop, calls=%fused_computation | loop fusion | flops 524288 | bytes 4194304 | tf_op jit(solution)/shard_map/mul | solution.py:482

commit v4 on v3

--- a/solution.py
+++ b/solution.py
@@ -19,7 +19,7 @@
 
 
 def kernel(pool_ref, ids_ref, rows_ref, w_hbm, eb_ref, db_ref, out_ref,
-           pos_ref, w_vm, cent, pcodes, codes, ybuf, xsend, xbuf, zsend, zbuf, sel, chosen,
+           hot_ref, w_vm, cent, pcodes, codes, ybuf, xsend, xbuf, zsend, zbuf, sel, chosen,
            w_sem, go, l_sem, ps, pr, cs, cr, ys, yr, xs, xr, qs, qr, rs, rr, zs, zr, fs, fr, ks, kr):
     r = lax.axis_index("rep")
     w = lax.axis_index("wide")
@@ -48,15 +48,6 @@
             cent[0, y, zl, x] = centered
         else:
             cent[1, x, zl, y] = centered
-
-    for n in range(TOK // 128):
-        ids = ids_ref[n * 128:(n + 1) * 128].reshape(1, 128)
-        ab, wp = (ids // 16) % 2, ids // 32
-        z_, y_, x_ = wp // 16, (wp // 4) % 4, wp % 4
-        k_ = jnp.where(ab == 0, y_, x_)
-        m_ = jnp.where(ab == 0, x_, y_)
-        place = ab * 512 + k_ * 128 + z_ * 64 + m_ * 16 + ids % 16
-        pos_ref[n * 128:(n + 1) * 128, :] = jnp.broadcast_to(place, (128, 128)).T
 
     pl.semaphore_wait(barrier, len(partners))
 
@@ -136,6 +127,7 @@
                         s = 7 + i * 8 + i * 4 + dm % 4
                         got(ab, piece(ab, -d, i, dm), s, second(ab, -d))
                         put(ab, piece(ab, -d, i, dm), 23 + i * 4 + dm % 4, second(ab, d))
+                yield 4
             for i, d in enumerate(steps):
                 for ab in range(2):
                     for dm in order:
@@ -192,7 +184,7 @@
             while next(task) != mark:
                 pass
 
-        def encode(d):
+        def encode(d, tiles=(0, 4)):
             ky, kx = (y + d + 4) % 4, (x + d + 4) % 4
 
             def tile(n, carry):
@@ -205,12 +197,29 @@
                 pcodes[pl.ds(pl.multiple_of(512 + kx * 128, 128), 128), cols] = made[128:]
                 return carry
 
-            lax.fori_loop(0, 4, tile, 0)
+            lax.fori_loop(*tiles, tile, 0)
+
+        def mark(n, carry):
+            at = pl.ds(pl.multiple_of(n * 128, 128), 128)
+            ids = ids_ref[at].reshape(1, 128)
+            ab, wp = (ids // 16) % 2, ids // 32
+            z_, y_, x_ = wp // 16, (wp // 4) % 4, wp % 4
+            k_ = jnp.where(ab == 0, y_, x_)
+            m_ = jnp.where(ab == 0, x_, y_)
+            place_of = ab * 512 + k_ * 128 + z_ * 64 + m_ * 16 + ids % 16
+            place_of = jnp.broadcast_to(place_of, (128, 128)).T
+            lane = lax.broadcasted_iota(jnp.int32, (128, 128), 1)
+            for j in range(8):
+                hot_ref[at, j * 128:(j + 1) * 128] = (place_of == lane + 128 * j).astype(F32).astype(BF16)
+            return carry
 
         rows = gather_rows(None if c == 0 else lambda: pl.semaphore_wait(go, 1))
         until(rows, 3)
         w_copy.wait()
-        encode(0)
+        for n in range(4):
+            next(rows)
+            encode(0, (n, n + 1))
+        lax.fori_loop(0, TOK // 128, mark, 0)
         until(rows, 5)
         encode(-1)
         until(rows, 6)
@@ -236,12 +245,8 @@
         def pick(i, carry):
             q = (i % 2) * 2 + i // 2
             at = pl.ds(pl.multiple_of(q * CHUNK, CHUNK), CHUNK)
-            place_of = pos_ref[at, :]
-            lane = lax.broadcasted_iota(jnp.int32, (CHUNK, 128), 1)
-            hot = jnp.concatenate(
-                [(place_of == lane + 128 * n).astype(F32) for n in range(8)], axis=1).astype(BF16)
             for half in range(2):
-                got = jnp.dot(hot, pcodes[:, half * HALF:(half + 1) * HALF], preferred_element_type=F32)
+                got = jnp.dot(hot_ref[at, :], pcodes[:, half * HALF:(half + 1) * HALF], preferred_element_type=F32)
                 codes[r, half, at, :] = got.astype(BF16)
             return carry
 
@@ -377,9 +382,9 @@
             until(deal, 2)
             until(deal, 3)
             pass_on(0)
-            pass_on(1)
             pieces_arrived(0)
             until(spread[0], 2)
+            pass_on(1)
             pass_on(2)
             pass_on(3)
             until(spread[0], 4)
@@ -399,16 +404,17 @@
             until(deal, 0)
             for q in range(4):
                 to_twin(0, q)
+            until(deal, 1)
+            along_z(1)
+            until(deal, 2)
             pieces_arrived(0)
             until(spread[0], 1)
-            until(deal, 1)
-            along_z(1)
-            until(spread[0], 2)
-            until(deal, 2)
             until(deal, 3)
             along_z(2)
             along_z(3)
+            until(spread[0], 2)
             pass_on(0)
+            until(spread[0], 3)
             pass_on(1)
             until(spread[0], 4)
             twin_arrived(0)
@@ -453,7 +459,7 @@
         in_specs=[vmem, vmem, smem, pl.BlockSpec(memory_space=pl.ANY), vmem, vmem],
         out_specs=vmem,
         scratch_shapes=[
-            pltpu.VMEM((TOK, 128), jnp.int32),
+            pltpu.VMEM((TOK, 1024), BF16),
             pltpu.VMEM((D, PANEL), BF16),
             pltpu.VMEM((2, 4, 2, 4, 16, D), BF16),
             pltpu.VMEM((1024, PANEL), BF16),

time: 173 us -> 172 us (level)
  no operation moved by 1% of the time
where the time goes in v4:
time: 172 us
  Pallas kernels  169 us (98%)
  other arithmetic  3.29 us (2%)
    pallas_call x1, Pallas kernels, local(): pl.pallas_call(kernel, out_shape=jax.ShapeDtypeStruct((ROWS, PANEL), F32)...  169 us

profile of v4, /device:TPU:2, one launch (start us, length us, event | category | flops | bytes accessed | tf_op | source)
XLA Modules:
  0.0 172.2 jit_solution(12918588301713862266)
XLA Ops:
  0.0 168.9 %shard_map.64 = f32[512,1024]{1,0:T(8,128)} custom-call(bf16[32,4096]{1,0:T(8,128)(2,1)} %pool_ref.1, s32[768]{0:T(1024)} %ids_ref.1, s32[2]{0:T(128)} %rows_ref.1, bf16[4096,1024]{1,0:T(8,128)(2,1)} %w_hbm.1, f32[1,1024]{1,0:T(1,128)} %bitcast.3, f32[1,4096]{1,0:T(1,128)} %bitcast.2), custom_call_target="tpu_custom_call" | custom-call | tf_op jit(solution)/shard_map/pallas_call | solution.py:456
  168.9 3.3 %broadcast_multiply_fusion = f32[512,1024]{1,0:T(8,128)} fusion(f32[512,1024]{1,0:T(8,128)} %shard_map.64), kind=kLoop, calls=%fused_computation | loop fusion | flops 524288 | bytes 4194304 | tf_op jit(solution)/shard_map/mul | solution.py:488

commit v5 on v4

--- a/solution.py
+++ b/solution.py
@@ -258,8 +258,8 @@
             part = chunk(rep_of((0, -1, 1, 2)[k], c), q)
             send(part, part, ks.at[k, q], kr.at[k, q], twin)
 
-        def twin_arrived(k):
-            for q in range(4):
+        def twin_arrived(k, chunks=(0, 1, 2, 3)):
+            for q in chunks:
                 arrived(chunk(rep_of((0, -1, 1, 2)[k], 1 - c), q), ks.at[k, q], kr.at[k, q], twin)
 
         def pass_on(q):
@@ -275,8 +275,8 @@
                 send(got, got, fs.at[1, q], fr.at[1, q], down)
             to_twin(2, p)
 
-        def far_codes():
-            for q in range(2):
+        def far_codes(pairs=(0, 1)):
+            for q in pairs:
                 arrived(chunk(rep_of(2, c), q), fs.at[0, q], fr.at[0, q], down)
                 to_twin(3, q)
                 arrived(chunk(rep_of(2, c), q + 2), fs.at[1, q], fr.at[1, q], up)
@@ -344,21 +344,23 @@
                     arrived(chosen.at[at + (zl, hs % 2)], rs.at[0, i], rr.at[0, i], (src, w))
                 arrived(chosen.at[at + (1 - zl, hs % 2)], rs.at[1, i], rr.at[1, i], (src, other[1]))
 
-        def gram(d, par, first=False):
+        def gram(d, par, first=False, chunks=(0, 1, 2, 3)):
             hs = (h + d + 4) % 4
             ab, slot = hs // 2, hs % 2
             rep = hs * 2 + par
 
             def quarter(qc, carry):
                 parts = []
-                for t in range(16):
+                for t in [4 * q + n for q in chunks for n in range(4)]:
                     k = jnp.where(ab == 0, t // 4, t % 4)
                     m = jnp.where(ab == 0, t % 4, t // 4)
                     parts.append(chosen[par, ab, k, m, qc, slot])
                 lhs = jnp.concatenate(parts, axis=0)
                 at = pl.ds(pl.multiple_of(qc * 256, 256), 256)
                 for half in range(2):
-                    made = lax.dot_general(lhs, codes[rep, half], (((0,), (0,)), ((), ())),
+                    rhs = jnp.concatenate(
+                        [codes[rep, half, q * CHUNK:(q + 1) * CHUNK, :] for q in chunks], axis=0)
+                    made = lax.dot_general(lhs, rhs, (((0,), (0,)), ((), ())),
                                            preferred_element_type=F32)
                     cols = slice(half * HALF, (half + 1) * HALF)
                     if first:
@@ -397,9 +399,12 @@
             until(spread[1], 3)
             gram(2, 0)
             until(spread[1], 4)
-            for k, d in enumerate((0, -1, 1, 2)):
+            for k, d in enumerate((0, -1, 1)):
                 twin_arrived(k)
                 gram(d, 1)
+            for pair in ((0, 2), (1, 3)):
+                twin_arrived(3, pair)
+                gram(2, 1, chunks=pair)
         else:
             until(deal, 0)
             for q in range(4):
@@ -434,8 +439,10 @@
             gram(1, 1)
             twin_arrived(3)
             gram(2, 0)
-            far_codes()
-            gram(2, 1)
+            far_codes((0,))
+            gram(2, 1, chunks=(0, 2))
+            far_codes((1,))
+            gram(2, 1, chunks=(1, 3))
 
         for d in sends:
             d.wait_send()

time: 172 us -> 172 us (level)
  no operation moved by 1% of the time
where the time goes in v5:
time: 172 us
  Pallas kernels  169 us (98%)
  other arithmetic  3.29 us (2%)
    pallas_call x1, Pallas kernels, local(): pl.pallas_call(kernel, out_shape=jax.ShapeDtypeStruct((ROWS, PANEL), F32)...  169 us

profile of v5, /device:TPU:2, one launch (start us, length us, event | category | flops | bytes accessed | tf_op | source)
XLA Modules:
  0.0 171.9 jit_solution(17127515033740328587)
XLA Ops:
  0.0 168.6 %shard_map.64 = f32[512,1024]{1,0:T(8,128)} custom-call(bf16[32,4096]{1,0:T(8,128)(2,1)} %pool_ref.1, s32[768]{0:T(1024)} %ids_ref.1, s32[2]{0:T(128)} %rows_ref.1, bf16[4096,1024]{1,0:T(8,128)(2,1)} %w_hbm.1, f32[1,1024]{1,0:T(1,128)} %bitcast.3, f32[1,4096]{1,0:T(1,128)} %bitcast.2), custom_call_target="tpu_custom_call" | custom-call | tf_op jit(solution)/shard_map/pallas_call | solution.py:463
  168.6 3.3 %broadcast_multiply_fusion = f32[512,1024]{1,0:T(8,128)} fusion(f32[512,1024]{1,0:T(8,128)} %shard_map.64), kind=kLoop, calls=%fused_computation | loop fusion | flops 524288 | bytes 4194304 | tf_op jit(solution)/shard_map/mul | solution.py:495
